TPU v7x, 256 devices: a whole 4x4x8 slice. The times are simulated.
256 devices in a mesh: inp: 8 (over z), wgt: 8 (over x_lo, y), out: 4 (over x_hi, core).
Axes of the slice: x: 4 (x_hi: 2, x_lo: 2; x = x_hi * 2 + x_lo), y: 4, z: 8, core: 2. Of those that a mesh axis runs over, the one named last changes fastest.
Arguments:
- tokens: bfloat16 [1024, 6144], P('out', ('wgt', 'inp')), may hold values from -6 to 6
- w_up: bfloat16 [6144, 24576], P(('wgt', 'out'), 'inp'), may hold values from -0.078125 to 0.078125
- w_down: bfloat16 [24576, 6144], P(('inp', 'out'), 'wgt'), may hold values from -0.0390625 to 0.0390625
- grad_out: bfloat16 [1024, 6144], P('out', ('wgt', 'inp')), may hold values from -6 to 6
Outputs:
- output: bfloat16 [1024, 6144], P('out', ('wgt', 'inp'))
- grad_tokens: bfloat16 [1024, 6144], P('out', ('wgt', 'inp'))
- grad_up: bfloat16 [6144, 24576], P(('wgt', 'out'), 'inp')
- grad_down: bfloat16 [24576, 6144], P(('inp', 'out'), 'wgt')
All inputs are finite; a program needn't handle non-finite values.
Results may differ from a plain program's by a relative error of at most 0.029.
Values may be sent and summed in bfloat16 or wider, within the bound.
No kernel may reach another device: no remote copies, remote signals or barrier semaphores. Data moves between devices by JAX's collectives and lax.ppermute only.
A program may use at most 64 MiB of HBM per device.

v0:
```python
import jax
import jax.numpy as jnp
from jax import lax
from jax.sharding import PartitionSpec as P

tanh_scale = 0.7978845608028654
cubic_weight = 0.044715


def gelu_value(hidden):
    tangent = jnp.tanh(tanh_scale * (hidden + cubic_weight * hidden * hidden * hidden))
    return 0.5 * hidden * (1.0 + tangent)


def gelu_slope(hidden):
    tangent = jnp.tanh(tanh_scale * (hidden + cubic_weight * hidden * hidden * hidden))
    return 0.5 * (1.0 + tangent) + 0.5 * hidden * (1.0 - tangent * tangent) * tanh_scale * (
        1.0 + 3.0 * cubic_weight * hidden * hidden
    )


def product(former, latter):
    return jnp.dot(former, latter, preferred_element_type=jnp.float32)


def against(former, latter):
    return lax.dot_general(
        former, latter, (((1,), (1,)), ((), ())), preferred_element_type=jnp.float32
    )


def across(former, latter):
    return lax.dot_general(
        former, latter, (((0,), (0,)), ((), ())), preferred_element_type=jnp.float32
    )


def share_features(partial_value):
    return lax.psum_scatter(
        partial_value.astype(jnp.bfloat16), "inp", scatter_dimension=1, tiled=True
    ).astype(jnp.float32)


def share_hidden(partial_value):
    return lax.psum_scatter(
        partial_value.astype(jnp.bfloat16), "wgt", scatter_dimension=1, tiled=True
    ).astype(jnp.float32)


def whole_hidden(portion):
    return lax.all_gather(portion, "wgt", axis=1, tiled=True)


def weight_grad(former, latter):
    return lax.psum_scatter(
        across(former, latter).astype(jnp.bfloat16), "out", scatter_dimension=0, tiled=True
    ).astype(jnp.float32)


def per_device(tokens, w_up, w_down, grad_out):
    features, grad_features = (
        lax.all_gather(tokens, "inp", axis=1, tiled=True),
        lax.all_gather(grad_out, "inp", axis=1, tiled=True),
    )
    up_block, down_block = (
        lax.all_gather(w_up, "out", axis=0, tiled=True),
        lax.all_gather(w_down, "out", axis=0, tiled=True),
    )
    hidden_partial = product(features, up_block)
    hidden = share_hidden(hidden_partial)
    activation = whole_hidden(gelu_value(hidden).astype(jnp.bfloat16))
    output = share_features(product(activation, down_block)).astype(jnp.bfloat16)
    up_again, down_again = (
        lax.all_gather(w_up, "out", axis=0, tiled=True),
        lax.all_gather(w_down, "out", axis=0, tiled=True),
    )
    act_partial = against(grad_features, down_again)
    grad_act = share_hidden(act_partial)
    grad_hidden = whole_hidden((grad_act * gelu_slope(hidden)).astype(jnp.bfloat16))
    grad_tokens = share_features(against(grad_hidden, up_again)).astype(jnp.bfloat16)
    grad_down = weight_grad(activation, grad_features).astype(jnp.bfloat16)
    grad_up = weight_grad(features, grad_hidden).astype(jnp.bfloat16)
    return (output, grad_tokens, grad_up, grad_down)


def solution(mesh):
    placed = (
        P("out", ("wgt", "inp")),
        P(("wgt", "out"), "inp"),
        P(("inp", "out"), "wgt"),
        P("out", ("wgt", "inp")),
    )
    return jax.shard_map(
        per_device,
        mesh=mesh,
        in_specs=placed,
        out_specs=(
            P("out", ("wgt", "inp")),
            P("out", ("wgt", "inp")),
            P(("wgt", "out"), "inp"),
            P(("inp", "out"), "wgt"),
        ),
        check_vma=False,
    )
```

profile of v0, /device:TPU:1, one launch (start us, length us, event | category | flops | bytes accessed | tf_op | source)
XLA Modules:
  0.0 491.5 jit_solution(3880922465054088078)
XLA Ops:
  8.7 23.7 %all_gather.24 = bf16[256,768]{0,1:T(8,128)(2,1)S(1)} all-gather(bf16[256,96]{0,1:T(8,128)(2,1)S(1)} %copy-done.2), channel_id=1, replica_groups=mesh['inp'=8,'wgt'=8,'out'=4] {'inp'}, dimensions={1}, use_global_device_ids=true | all-gather | bytes 442368 | tf_op jit(solution)/shard_map/all_gather | solution.py:63
  32.4 25.7 %all-gather.9.cloned.1.call-done = bf16[3072,768]{1,0:T(8,128)(2,1)} async-done(((bf16[768,768]{1,0:T(8,128)(2,1)}), bf16[3072,768]{1,0:T(8,128)(2,1)}) %all-gather.9.cloned.1.call-update) | async-done | bytes 4718608 | tf_op jit(solution)/shard_map/all_gather | solution.py:67
  58.1 3.8 convolution_convert_fusion.2
  61.9 1.6 copy.12
  64.3 21.4 %all_gather.20 = bf16[256,768]{0,1:T(8,128)(2,1)S(1)} all-gather(bf16[256,96]{0,1:T(8,128)(2,1)S(1)} %copy-done.3), channel_id=1, replica_groups=mesh['inp'=8,'wgt'=8,'out'=4] {'inp'}, dimensions={1}, use_global_device_ids=true | all-gather | bytes 442368 | tf_op jit(solution)/shard_map/all_gather | solution.py:62
  85.6 17.8 %all-gather.5.cloned.1.call-done = bf16[768,3072]{1,0:T(8,128)(2,1)} async-done(((bf16[192,3072]{1,0:T(8,128)(2,1)}), bf16[768,3072]{1,0:T(8,128)(2,1)}) %all-gather.5.cloned.1.call-update) | async-done | bytes 4718608 | tf_op jit(solution)/shard_map/all_gather | solution.py:66
  103.5 3.7 convolution_convert_fusion.3
  107.2 1.6 copy.10
  108.9 34.6 %reduce-scatter.21.cloned.1.call-done = bf16[384,256]{1,0:T(8,128)(2,1)} async-done(((bf16[3072,256]{1,0:T(8,128)(2,1)}), bf16[384,256]{1,0:T(8,128)(2,1)}) %reduce-scatter.21.cloned.1.call-update) | async-done | bytes 196624
  143.5 1.1 copy.13
  144.6 43.6 %reduce-scatter.19.cloned.1.call-done = bf16[384,256]{1,0:T(8,128)(2,1)} async-done(((bf16[3072,256]{1,0:T(8,128)(2,1)}), bf16[384,256]{1,0:T(8,128)(2,1)}) %reduce-scatter.19.cloned.1.call-update) | async-done | bytes 196624
  188.2 1.1 copy.11
  191.0 40.2 %all-gather.11.cloned.1.call-done = bf16[256,3072]{1,0:T(8,128)(2,1)} async-done(((bf16[256,384]{1,0:T(8,128)(2,1)}), bf16[256,3072]{1,0:T(8,128)(2,1)}) %all-gather.11.cloned.1.call-update) | async-done | bytes 1572880 | tf_op jit(solution)/shard_map/all_gather | solution.py:51
  231.2 5.0 %convolution_convert_fusion.4 = bf16[256,768]{0,1:T(8,128)(2,1)} fusion(bf16[256,3072]{1,0:T(8,128)(2,1)} %all-gather.11.cloned.1.call-done, bf16[768,3072]{1,0:T(8,128)(2,1)} %all-gather.5.cloned.1.call-done), kind=kOutput, calls=%fused_computation.5 | convolution fusion | flops 1208156160 | bytes 6684672 | tf_op jit(solution)/shard_map/dot_general | solution.py:27
  236.2 39.3 %all-gather.7.cloned.1.call-done = bf16[256,3072]{1,0:T(8,128)(2,1)} async-done(((bf16[256,384]{1,0:T(8,128)(2,1)}), bf16[256,3072]{1,0:T(8,128)(2,1)}) %all-gather.7.cloned.1.call-update) | async-done | bytes 1572880 | tf_op jit(solution)/shard_map/all_gather | solution.py:51
  275.5 5.6 %convolution_convert_fusion.5 = bf16[256,768]{0,1:T(8,128)(2,1)} fusion(bf16[256,3072]{1,0:T(8,128)(2,1)} %all-gather.7.cloned.1.call-done, bf16[3072,768]{1,0:T(8,128)(2,1)} %all-gather.9.cloned.1.call-done), kind=kOutput, calls=%fused_computation.6 | convolution fusion | flops 1208156160 | bytes 6684672 | tf_op jit(solution)/shard_map/dot_general | solution.py:23
  281.3 3.6 convolution_convert_fusion
  284.9 1.3 copy-done
  286.2 3.7 fusion
  289.9 6.7 %copy.14 = bf16[768,3072]{1,0:T(8,128)(2,1)} copy(bf16[768,3072]{0,1:T(8,128)(2,1)} %fusion) | data formatting | bytes 9437184
  296.7 19.6 %reduce-scatter.15.cloned.1.call-done = bf16[256,96]{0,1:T(8,128)(2,1)} async-done(((bf16[256,768]{0,1:T(8,128)(2,1)}), bf16[256,96]{0,1:T(8,128)(2,1)}) %reduce-scatter.15.cloned.1.call-update) | async-done | bytes 49168 | tf_op jit(solution)/shard_map/reduce_scatter | solution.py:39
  316.3 38.9 %reduce-scatter.13.cloned.1.call-done = bf16[256,96]{0,1:T(8,128)(2,1)} async-done(((bf16[256,768]{0,1:T(8,128)(2,1)}), bf16[256,96]{0,1:T(8,128)(2,1)}) %reduce-scatter.13.cloned.1.call-update) | async-done | bytes 49168 | tf_op jit(solution)/shard_map/reduce_scatter | solution.py:39
  355.2 66.7 %reduce-scatter.17.cloned.1.call-done = bf16[768,768]{1,0:T(8,128)(2,1)} async-done(((bf16[3072,768]{1,0:T(8,128)(2,1)}), bf16[768,768]{1,0:T(8,128)(2,1)}) %reduce-scatter.17.cloned.1.call-update) | async-done | bytes 1179664 | tf_op jit(solution)/shard_map/reduce_scatter | solution.py:55
  421.9 62.8 %reduce-scatter.23.cloned.1.call-done = bf16[192,3072]{1,0:T(8,128)(2,1)} async-done(((bf16[768,3072]{1,0:T(8,128)(2,1)}), bf16[192,3072]{1,0:T(8,128)(2,1)}) %reduce-scatter.23.cloned.1.call-update) | async-done | bytes 1179664
  (28 shorter events, 4.2 us)
Async XLA Ops:
  7.2 1.5 copy-start.2
  7.2 50.9 %all-gather.9.cloned.1.call-start = ((), (), s32[]{:S(2)}) async-start(), calls=%async_computation.8 | async-start | bytes 5898240 | tf_op jit(solution)/shard_map/all_gather | solution.py:67
  7.9 95.6 %all-gather.5.cloned.1.call-start = ((), (), s32[]{:S(2)}) async-start(), calls=%async_computation.6 | async-start | bytes 5898240 | tf_op jit(solution)/shard_map/all_gather | solution.py:66
  8.7 134.8 %reduce-scatter.21.cloned.1.call-start = ((), (), s32[]{:S(2)}) async-start(), calls=%async_computation.14 | async-start | bytes 1769472
  63.5 0.8 copy-start.3
  63.5 124.7 %reduce-scatter.19.cloned.1.call-start = ((), (), s32[]{:S(2)}) async-start(), calls=%async_computation.13 | async-start | bytes 1769472
  108.8 122.4 %all-gather.11.cloned.1.call-start = ((), (), s32[]{:S(2)}) async-start(), calls=%async_computation.10 | async-start | bytes 1769472 | tf_op jit(solution)/shard_map/all_gather | solution.py:51
  190.4 85.2 %all-gather.7.cloned.1.call-start = ((), (), s32[]{:S(2)}) async-start(), calls=%async_computation.7 | async-start | bytes 1769472 | tf_op jit(solution)/shard_map/all_gather | solution.py:51
  190.9 125.4 %reduce-scatter.15.cloned.1.call-start = ((), (), s32[]{:S(2)}) async-start(), calls=%async_computation.11 | async-start | bytes 442368 | tf_op jit(solution)/shard_map/reduce_scatter | solution.py:39
  236.2 119.1 %reduce-scatter.13.cloned.1.call-start = ((), (), s32[]{:S(2)}) async-start(), calls=%async_computation.9 | async-start | bytes 442368 | tf_op jit(solution)/shard_map/reduce_scatter | solution.py:39
  275.5 5.7 %copy-start.1 = (bf16[256,3072]{1,0:T(8,128)(2,1)S(1)}, bf16[256,3072]{1,0:T(8,128)(2,1)}, u32[]{:S(2)}) copy-start(bf16[256,3072]{1,0:T(8,128)(2,1)} %all-gather.7.cloned.1.call-done) | copy-start | bytes 4718596
  281.2 140.7 %reduce-scatter.17.cloned.1.call-start = ((), (), s32[]{:S(2)}) async-start(), calls=%async_computation.12 | async-start | bytes 5898240 | tf_op jit(solution)/shard_map/reduce_scatter | solution.py:55
  284.8 1.4 copy-start
  284.9 199.8 %reduce-scatter.23.cloned.1.call-start = ((), (), s32[]{:S(2)}) async-start(), calls=%async_computation.15 | async-start | bytes 5898240
Sparse Core Ops, SparseCore 0:
  9.8 48.2 all-gather.8
  59.9 43.5 all-gather.4
  106.0 37.3 reduce-scatter.20
  145.9 42.2 reduce-scatter.18
  190.5 40.6 all-gather.10
  233.4 42.0 all-gather.6
  278.6 37.6 reduce-scatter.14
  319.5 35.6 reduce-scatter.12
  358.6 63.2 reduce-scatter.16
  425.3 59.3 reduce-scatter.22
where the time goes:
time: 492 us
  waiting for transfers between devices  391 us (79%)
  blocking collectives  45.1 us (9%)
  matrix products  25.4 us (5%)
  between operations  14.2 us (3%)
  local copies, waits for them, and re-layouts  14.1 us (3%)
    unnamed x13, waiting for transfers between devices  143 us
    all_gather x2, waiting for transfers between devices, whole_hidden(): return lax.all_gather(portion, 'wgt', axis=1, tiled=True)  79.5 us
    reduce_scatter x1, waiting for transfers between devices, weight_grad(): lax.psum_scatter(across(former, latter).astype(jnp.bfloat16), 'out', scat...  66.7 us
    reduce_scatter x2, waiting for transfers between devices, share_features(): lax.psum_scatter(partial_value.astype(jnp.bfloat16), 'inp', scatter_dimen...  58.6 us
    all_gather x1, waiting for transfers between devices, per_device(): lax.all_gather(w_down, 'out', axis=0, tiled=True)  25.7 us
    all_gather x1, blocking collectives, per_device(): lax.all_gather(grad_out, 'inp', axis=1, tiled=True)  23.7 us
    all_gather x1, blocking collectives, per_device(): lax.all_gather(tokens, 'inp', axis=1, tiled=True)  21.4 us
    all_gather x1, waiting for transfers between devices, per_device(): lax.all_gather(w_up, 'out', axis=0, tiled=True)  17.8 us
  transfers between devices with their start and end apart: 10, of which 10 were waited for; matrix products, arithmetic and copies ran while one was open for 7% of the time, Pallas kernels for 0%

commit v1 on v0

--- a/solution.py
+++ b/solution.py
@@ -60,7 +60,9 @@
 def per_device(tokens, w_up, w_down, grad_out):
     features, grad_features = (
         lax.all_gather(tokens, "inp", axis=1, tiled=True),
-        lax.all_gather(grad_out, "inp", axis=1, tiled=True),
+        jnp.concatenate(
+            lax.all_to_all(jnp.stack([grad_out] * lax.axis_size("inp")), "inp", 0, 0), axis=1
+        ),
     )
     up_block, down_block = (
         lax.all_gather(w_up, "out", axis=0, tiled=True),

time: 492 us -> 492 us (level)
    all_gather x1 -> x0, blocking collectives: 23.7 us -> none  [per_device(): lax.all_gather(grad_out, 'inp', axis=1, tiled=True)]
    all_to_all x0 -> x1, blocking collectives: none -> 22.3 us  [per_device(): lax.all_to_all(jnp.stack([grad_out] * lax.axis_size('inp')), 'inp', 0, 0)]
where the time goes in v1:
time: 492 us
  waiting for transfers between devices  393 us (80%)
  blocking collectives  43.7 us (9%)
  matrix products  25.4 us (5%)
  between operations  14.2 us (3%)
  local copies, waits for them, and re-layouts  14.1 us (3%)
    unnamed x13, waiting for transfers between devices  143 us
    all_gather x2, waiting for transfers between devices, whole_hidden(): return lax.all_gather(portion, 'wgt', axis=1, tiled=True)  79.5 us
    reduce_scatter x1, waiting for transfers between devices, weight_grad(): lax.psum_scatter(across(former, latter).astype(jnp.bfloat16), 'out', scat...  66.7 us
    reduce_scatter x2, waiting for transfers between devices, share_features(): lax.psum_scatter(partial_value.astype(jnp.bfloat16), 'inp', scatter_dimen...  58.6 us
    all_gather x1, waiting for transfers between devices, per_device(): lax.all_gather(w_down, 'out', axis=0, tiled=True)  27 us
    all_to_all x1, blocking collectives, per_device(): lax.all_to_all(jnp.stack([grad_out] * lax.axis_size('inp')), 'inp', 0, 0)  22.3 us
    all_gather x1, blocking collectives, per_device(): lax.all_gather(tokens, 'inp', axis=1, tiled=True)  21.4 us
    all_gather x1, waiting for transfers between devices, per_device(): lax.all_gather(w_up, 'out', axis=0, tiled=True)  17.8 us
  transfers between devices with their start and end apart: 10, of which 10 were waited for; matrix products, arithmetic and copies ran while one was open for 7% of the time, Pallas kernels for 0%

profile of v1, /device:TPU:1, one launch (start us, length us, event | category | flops | bytes accessed | tf_op | source)
XLA Modules:
  0.0 491.5 jit_solution(1685771545222904754)
XLA Ops:
  8.7 22.3 %all_to_all.5 = bf16[8,256,96]{1,2,0:T(8,128)(2,1)S(1)} all-to-all(bf16[8,256,96]{1,2,0:T(8,128)(2,1)S(1)} %stack.2), channel_id=1, replica_groups=mesh['inp'=8,'wgt'=8,'out'=4] {'inp'}, dimensions={0} | all-to-all | bytes 786432 | tf_op jit(solution)/shard_map/all_to_all | solution.py:64
  31.1 27.0 %all-gather.9.cloned.1.call-done = bf16[3072,768]{1,0:T(8,128)(2,1)} async-done(((bf16[768,768]{1,0:T(8,128)(2,1)}), bf16[3072,768]{1,0:T(8,128)(2,1)}) %all-gather.9.cloned.1.call-update) | async-done | bytes 4718608 | tf_op jit(solution)/shard_map/all_gather | solution.py:69
  58.1 3.8 convolution_convert_fusion.2
  61.9 1.6 copy.14
  64.3 21.4 %all_gather.17 = bf16[256,768]{0,1:T(8,128)(2,1)S(1)} all-gather(bf16[256,96]{0,1:T(8,128)(2,1)S(1)} %copy-done.3), channel_id=1, replica_groups=mesh['inp'=8,'wgt'=8,'out'=4] {'inp'}, dimensions={1}, use_global_device_ids=true | all-gather | bytes 442368 | tf_op jit(solution)/shard_map/all_gather | solution.py:62
  85.6 17.8 %all-gather.5.cloned.1.call-done = bf16[768,3072]{1,0:T(8,128)(2,1)} async-done(((bf16[192,3072]{1,0:T(8,128)(2,1)}), bf16[768,3072]{1,0:T(8,128)(2,1)}) %all-gather.5.cloned.1.call-update) | async-done | bytes 4718608 | tf_op jit(solution)/shard_map/all_gather | solution.py:68
  103.5 3.7 convolution_convert_fusion.3
  107.2 1.6 copy.12
  108.9 34.6 %reduce-scatter.21.cloned.1.call-done = bf16[384,256]{1,0:T(8,128)(2,1)} async-done(((bf16[3072,256]{1,0:T(8,128)(2,1)}), bf16[384,256]{1,0:T(8,128)(2,1)}) %reduce-scatter.21.cloned.1.call-update) | async-done | bytes 196624
  143.5 1.1 copy.15
  144.6 43.6 %reduce-scatter.19.cloned.1.call-done = bf16[384,256]{1,0:T(8,128)(2,1)} async-done(((bf16[3072,256]{1,0:T(8,128)(2,1)}), bf16[384,256]{1,0:T(8,128)(2,1)}) %reduce-scatter.19.cloned.1.call-update) | async-done | bytes 196624
  188.2 1.1 copy.13
  191.0 40.2 %all-gather.11.cloned.1.call-done = bf16[256,3072]{1,0:T(8,128)(2,1)} async-done(((bf16[256,384]{1,0:T(8,128)(2,1)}), bf16[256,3072]{1,0:T(8,128)(2,1)}) %all-gather.11.cloned.1.call-update) | async-done | bytes 1572880 | tf_op jit(solution)/shard_map/all_gather | solution.py:51
  231.2 5.0 %convolution_convert_fusion.4 = bf16[256,768]{0,1:T(8,128)(2,1)} fusion(bf16[256,3072]{1,0:T(8,128)(2,1)} %all-gather.11.cloned.1.call-done, bf16[768,3072]{1,0:T(8,128)(2,1)} %all-gather.5.cloned.1.call-done), kind=kOutput, calls=%fused_computation.5 | convolution fusion | flops 1208156160 | bytes 6684672 | tf_op jit(solution)/shard_map/dot_general | solution.py:27
  236.2 39.3 %all-gather.7.cloned.1.call-done = bf16[256,3072]{1,0:T(8,128)(2,1)} async-done(((bf16[256,384]{1,0:T(8,128)(2,1)}), bf16[256,3072]{1,0:T(8,128)(2,1)}) %all-gather.7.cloned.1.call-update) | async-done | bytes 1572880 | tf_op jit(solution)/shard_map/all_gather | solution.py:51
  275.5 5.6 %convolution_convert_fusion.5 = bf16[256,768]{0,1:T(8,128)(2,1)} fusion(bf16[256,3072]{1,0:T(8,128)(2,1)} %all-gather.7.cloned.1.call-done, bf16[3072,768]{1,0:T(8,128)(2,1)} %all-gather.9.cloned.1.call-done), kind=kOutput, calls=%fused_computation.6 | convolution fusion | flops 1208156160 | bytes 6684672 | tf_op jit(solution)/shard_map/dot_general | solution.py:23
  281.3 3.6 convolution_convert_fusion
  284.9 1.3 copy-done
  286.2 3.7 fusion
  289.9 6.7 %copy.16 = bf16[768,3072]{1,0:T(8,128)(2,1)} copy(bf16[768,3072]{0,1:T(8,128)(2,1)} %fusion) | data formatting | bytes 9437184
  296.7 19.6 %reduce-scatter.15.cloned.1.call-done = bf16[256,96]{0,1:T(8,128)(2,1)} async-done(((bf16[256,768]{0,1:T(8,128)(2,1)}), bf16[256,96]{0,1:T(8,128)(2,1)}) %reduce-scatter.15.cloned.1.call-update) | async-done | bytes 49168 | tf_op jit(solution)/shard_map/reduce_scatter | solution.py:39
  316.3 38.9 %reduce-scatter.13.cloned.1.call-done = bf16[256,96]{0,1:T(8,128)(2,1)} async-done(((bf16[256,768]{0,1:T(8,128)(2,1)}), bf16[256,96]{0,1:T(8,128)(2,1)}) %reduce-scatter.13.cloned.1.call-update) | async-done | bytes 49168 | tf_op jit(solution)/shard_map/reduce_scatter | solution.py:39
  355.2 66.7 %reduce-scatter.17.cloned.1.call-done = bf16[768,768]{1,0:T(8,128)(2,1)} async-done(((bf16[3072,768]{1,0:T(8,128)(2,1)}), bf16[768,768]{1,0:T(8,128)(2,1)}) %reduce-scatter.17.cloned.1.call-update) | async-done | bytes 1179664 | tf_op jit(solution)/shard_map/reduce_scatter | solution.py:55
  421.9 62.8 %reduce-scatter.23.cloned.1.call-done = bf16[192,3072]{1,0:T(8,128)(2,1)} async-done(((bf16[768,3072]{1,0:T(8,128)(2,1)}), bf16[192,3072]{1,0:T(8,128)(2,1)}) %reduce-scatter.23.cloned.1.call-update) | async-done | bytes 1179664
  (29 shorter events, 4.2 us)
Async XLA Ops:
  7.2 1.5 copy-start.2
  7.2 50.9 %all-gather.9.cloned.1.call-start = ((), (), s32[]{:S(2)}) async-start(), calls=%async_computation.9 | async-start | bytes 5898240 | tf_op jit(solution)/shard_map/all_gather | solution.py:69
  7.9 95.6 %all-gather.5.cloned.1.call-start = ((), (), s32[]{:S(2)}) async-start(), calls=%async_computation.7 | async-start | bytes 5898240 | tf_op jit(solution)/shard_map/all_gather | solution.py:68
  8.7 134.8 %reduce-scatter.21.cloned.1.call-start = ((), (), s32[]{:S(2)}) async-start(), calls=%async_computation.15 | async-start | bytes 1769472
  63.5 0.8 copy-start.3
  63.5 124.7 %reduce-scatter.19.cloned.1.call-start = ((), (), s32[]{:S(2)}) async-start(), calls=%async_computation.14 | async-start | bytes 1769472
  108.8 122.4 %all-gather.11.cloned.1.call-start = ((), (), s32[]{:S(2)}) async-start(), calls=%async_computation.11 | async-start | bytes 1769472 | tf_op jit(solution)/shard_map/all_gather | solution.py:51
  190.4 85.2 %all-gather.7.cloned.1.call-start = ((), (), s32[]{:S(2)}) async-start(), calls=%async_computation.8 | async-start | bytes 1769472 | tf_op jit(solution)/shard_map/all_gather | solution.py:51
  190.9 125.4 %reduce-scatter.15.cloned.1.call-start = ((), (), s32[]{:S(2)}) async-start(), calls=%async_computation.12 | async-start | bytes 442368 | tf_op jit(solution)/shard_map/reduce_scatter | solution.py:39
  236.2 119.1 %reduce-scatter.13.cloned.1.call-start = ((), (), s32[]{:S(2)}) async-start(), calls=%async_computation.10 | async-start | bytes 442368 | tf_op jit(solution)/shard_map/reduce_scatter | solution.py:39
  275.5 5.7 %copy-start.1 = (bf16[256,3072]{1,0:T(8,128)(2,1)S(1)}, bf16[256,3072]{1,0:T(8,128)(2,1)}, u32[]{:S(2)}) copy-start(bf16[256,3072]{1,0:T(8,128)(2,1)} %all-gather.7.cloned.1.call-done) | copy-start | bytes 4718596
  281.2 140.7 %reduce-scatter.17.cloned.1.call-start = ((), (), s32[]{:S(2)}) async-start(), calls=%async_computation.13 | async-start | bytes 5898240 | tf_op jit(solution)/shard_map/reduce_scatter | solution.py:55
  284.8 1.4 copy-start
  284.9 199.8 %reduce-scatter.23.cloned.1.call-start = ((), (), s32[]{:S(2)}) async-start(), calls=%async_computation.16 | async-start | bytes 5898240
Sparse Core Ops, SparseCore 0:
  9.8 48.2 all-gather.8
  59.9 43.5 all-gather.4
  106.0 37.3 reduce-scatter.20
  145.9 42.2 reduce-scatter.18
  190.5 40.6 all-gather.10
  233.4 42.0 all-gather.6
  278.6 37.6 reduce-scatter.14
  319.5 35.6 reduce-scatter.12
  358.6 63.2 reduce-scatter.16
  425.3 59.3 reduce-scatter.22
